TPU v7x, 32 devices: a whole 2x2x4 slice. The times are simulated.
32 devices in a mesh: row: 4 (over y, x), col: 8 (over z, core).
Axes of the slice: x: 2, y: 2, z: 4, core: 2. Of those that a mesh axis runs over, the one named last changes fastest.
Arguments:
- points: int32 [16, 3, 1024], P('row', None, 'col'), may hold values from 0 to 31
- ranks: int32 [16], replicated, may hold values from 64 to 256, as said below
- bases: bfloat16 [16, 1024, 256], P('row', 'col'), may hold values from -0.375 to 0.375
- pivots: bfloat16 [2, 256, 256], replicated, may hold values from -0.119628906 to 0.119628906
- probes: bfloat16 [16, 64, 1024], P('col'), may hold values from -0.119628906 to 0.119628906
Outputs:
- updated: bfloat16 [16, 16, 256, 256], P('row', 'col')
- images: float32 [16, 64, 1024], P('row', None, 'col')
Inputs may be any that keep to these rules, and one draw needn't show every extreme that they name: `ranks`: the rank of each tile; some tile has rank 256 and some rank 256 // 4.
All inputs are finite; a program needn't handle non-finite values.
Results may differ from a plain program's by a relative error of at most 0.004.
The roundings to bfloat16 on the way count: a program that leaves them out, or rounds other values in their place, can miss the bound.
Values may be sent and summed in bfloat16 or wider, within the bound.
A program may use at most 64 MiB of HBM per device.

v0:
```python
import jax
import jax.numpy as jnp
from jax import lax
from jax.sharding import PartitionSpec as P

B = 1024
R = 256
PANELS = 2
nugget = 0.25
decay_length = 4.0
wave_length = 3.0


def spread(x, axis, root):
    mine = lax.axis_index(axis) == root
    return lax.psum(jnp.where(mine, x, jnp.zeros_like(x)), axis)


def kernel_block(rows, cols):
    diff = rows[:, :, None] - cols[:, None, :]
    dist = jnp.sqrt(jnp.sum(diff * diff, axis=0) + nugget)
    return (jnp.exp(-dist / decay_length) * jnp.cos(dist / wave_length)).astype(jnp.bfloat16)


def body(points, ranks, bases, pivots, probes):
    row_count = bases.shape[0]
    col_count = probes.shape[0]
    row_index = lax.axis_index("row")
    col_index = lax.axis_index("col")
    row_bases, row_points = (
        lax.all_gather(bases, "col", axis=1, tiled=True),
        lax.all_gather(points.astype(jnp.bfloat16), "col", axis=2, tiled=True),
    )
    root = col_index * col_count // row_count
    offset = col_index * col_count - root * row_count
    picked_bases = lax.dynamic_slice_in_dim(row_bases, offset, col_count, 0)
    picked_points = lax.dynamic_slice_in_dim(row_points, offset, col_count, 0)
    col_bases, col_points = (spread(picked_bases, "row", root), spread(picked_points, "row", root))
    col_coords = col_points.astype(jnp.float32)
    block = min(B, 256)
    nblocks = B // block

    def row_tile(item):
        tile_points, tile_bases = item
        coords = tile_points.astype(jnp.float32).reshape(3, nblocks, block).transpose(1, 0, 2)
        basis_blocks = tile_bases.reshape(nblocks, block, R)

        def add_block(total, blk):
            block_points, block_bases = blk
            tiles = jax.vmap(lambda other: kernel_block(block_points, other))(col_coords)
            proj = jnp.einsum(
                "jnm,jmr->jnr", tiles, col_bases, preferred_element_type=jnp.float32
            ).astype(jnp.bfloat16)
            return (
                total
                + jnp.einsum("nr,jns->jrs", block_bases, proj, preferred_element_type=jnp.float32),
                None,
            )

        total, _ = lax.scan(
            add_block, jnp.zeros((col_count, R, R), jnp.float32), (coords, basis_blocks)
        )
        return total

    raw = lax.map(row_tile, (row_points, row_bases))
    rank_iota = jnp.arange(R, dtype=jnp.int32)
    row_ranks = lax.dynamic_slice_in_dim(ranks, row_index * row_count, row_count)
    col_ranks = lax.dynamic_slice_in_dim(ranks, col_index * col_count, col_count)
    row_mask = (rank_iota[None, :] < row_ranks[:, None]).astype(jnp.float32)
    col_mask = (rank_iota[None, :] < col_ranks[:, None]).astype(jnp.float32)
    cores = (raw * row_mask[:, None, :, None] * col_mask[None, :, None, :]).astype(jnp.bfloat16)
    row_panel = spread(cores, "col", 0)
    col_panel = spread(cores[:PANELS], "row", 0)
    left = jnp.einsum(
        "ikab,kbc->ikac", row_panel, pivots, preferred_element_type=jnp.float32
    ).astype(jnp.bfloat16)
    update = jnp.einsum("ikac,kjcd->ijad", left, col_panel, preferred_element_type=jnp.float32)
    row_ids = row_index * row_count + jnp.arange(row_count, dtype=jnp.int32)
    col_ids = col_index * col_count + jnp.arange(col_count, dtype=jnp.int32)
    trailing = (row_ids >= PANELS)[:, None] & (col_ids >= PANELS)[None, :]
    updated = (
        cores.astype(jnp.float32) - jnp.where(trailing[:, :, None, None], update, 0.0)
    ).astype(jnp.bfloat16)
    probe_cores = jnp.einsum(
        "jpn,jnr->jpr", probes, col_bases, preferred_element_type=jnp.float32
    ).astype(jnp.bfloat16)
    partial_cores = jnp.einsum(
        "ijab,jpb->ipa", updated, probe_cores, preferred_element_type=jnp.float32
    )
    summed = lax.psum(partial_cores, "col")
    images = jnp.einsum(
        "ipa,ina->ipn", summed, bases.astype(jnp.float32), precision=lax.Precision.HIGHEST
    )
    return (updated, images)


def solution(mesh):
    placed = (P("row", None, "col"), P(), P("row", "col", None), P(), P("col", None, None))
    return jax.shard_map(
        body,
        mesh=mesh,
        in_specs=placed,
        out_specs=(P("row", "col", None, None), P("row", None, "col")),
        check_vma=False,
    )
```

profile of v0, /device:TPU:0, one launch (start us, length us, event | category | flops | bytes accessed | tf_op | source)
XLA Modules:
  0.0 444.0 jit_solution(3983174135087618088)
XLA Ops:
  8.0 33.5 %all-gather.2.cloned.1.call-done = bf16[4,1024,256]{2,1,0:T(8,128)(2,1)} async-done(((bf16[4,128,256]{2,1,0:T(8,128)(2,1)}), bf16[4,1024,256]{2,1,0:T(8,128)(2,1)}) %all-gather.2.cloned.1.call-update) | async-done | bytes 2097168 | tf_op jit(solution)/shard_map/all_gather | solution.py:31
  41.5 2.3 dynamic-slice_select_fusion
  43.9 10.4 %all_gather.6 = bf16[4,3,1024]{2,0,1:T(4,128)(2,1)S(1)} all-gather(bf16[4,3,128]{2,0,1:T(4,128)(2,1)S(1)} %convert_element_type.53), channel_id=1, replica_groups=mesh['row'=4,'col'=8] {'col'}, dimensions={2}, use_global_device_ids=true | all-gather | bytes 27648 | tf_op jit(solution)/shard_map/all_gather | solution.py:32
  54.3 16.0 %psum.35 = bf16[2,3,1024]{2,0,1:T(2,128)(2,1)S(1)} all-reduce(bf16[2,3,1024]{2,0,1:T(2,128)(2,1)S(1)} %broadcast_select_fusion.1), channel_id=1, replica_groups=mesh['row'=4,'col'=8] {'row'}, use_global_device_ids=true, to_apply=%region_0.1 | all-reduce | flops 6144 | bytes 24576 | tf_op jit(solution)/shard_map/psum | solution.py:16
  70.6 26.7 %all-reduce.5.cloned.1.call-done = bf16[2,1024,256]{2,1,0:T(8,128)(2,1)} async-done(((bf16[2,1024,256]{2,1,0:T(8,128)(2,1)}), bf16[2,1024,256]{2,1,0:T(8,128)(2,1)}) %all-reduce.5.cloned.1.call-update) | async-done | bytes 1048592 | tf_op jit(solution)/shard_map/psum | solution.py:16
  97.3 168.2 %while.25 = (s32[]{:T(128)}, f32[4,2,256,256]{3,2,1,0:T(8,128)}, bf16[4,3,1024]{2,1,0:T(4,128)(2,1)S(1)}, bf16[4,1024,256]{2,1,0:T(8,128)(2,1)}, f32[2,3,1024]{2...) while((s32[]{:T(128)}, f32[4,2,256,256]{3,2,1,0:T(8,128)}, ...), condition=%wide.region_6.7_spmd.clone, body=%wide.region_2.6_spmd.sunk.clone | while | flops 343280640 | bytes 9633548 | solution.py:65
  98.4 39.9 %while.24 = (s32[]{:T(128)}, f32[2,256,256]{1,2,0:T(8,128)S(1)}, f32[4,3,256]{2,1,0:T(4,128)S(1)}, f32[2,3,1024]{2,1,0:T(4,128)S(1)}, bf16[2,1024,256]{2,1,0:T(8...) while((s32[]{:T(128)}, f32[2,256,256]{1,2,0:T(8,128)S(1)}, ...), condition=%wide.region_5.5_spmd.clone, body=%wide.region_3.4_spmd.clone.sunk | while | flops 343277568 | bytes 6456423 | solution.py:60
  99.1 9.3 %fusion.31 = f32[2,256,256]{1,2,0:T(8,128)S(1)} fusion(bf16[2,1024,256]{2,1,0:T(8,128)(2,1)} %get-tuple-element.269, f32[2,256,1024]{2,1,0:T(8,128)S(1)} %multiply_reduce_fusion.2, f32[2,256,256]{1,2,0:T(8,128)S(1)} %get-tuple-element.258, pred[]{:T(512)S(6)} %compare.5, bf16[4,256,256]{2,1,0:T(8,128)(2,1)S(1)} %get-tuple-element.270, ...), kind=kOutput, calls=%fused_computation.3.clone.1 | convolution fusion | flops 339083264 | bytes 4325381 | tf_op jit(solution)/shard_map/while/body/eval_jaxpr/while/body/eval_jaxpr/nr,jns->jrs/dot_general | solution.py:56
  109.1 9.3 %fusion.31 = f32[2,256,256]{1,2,0:T(8,128)S(1)} fusion(bf16[2,1024,256]{2,1,0:T(8,128)(2,1)} %get-tuple-element.269, f32[2,256,1024]{2,1,0:T(8,128)S(1)} %multiply_reduce_fusion.2, f32[2,256,256]{1,2,0:T(8,128)S(1)} %get-tuple-element.258, pred[]{:T(512)S(6)} %compare.5, bf16[4,256,256]{2,1,0:T(8,128)(2,1)S(1)} %get-tuple-element.270, ...), kind=kOutput, calls=%fused_computation.3.clone.1 | convolution fusion | flops 339083264 | bytes 4325381 | tf_op jit(solution)/shard_map/while/body/eval_jaxpr/while/body/eval_jaxpr/nr,jns->jrs/dot_general | solution.py:56
  119.1 9.3 %fusion.31 = f32[2,256,256]{1,2,0:T(8,128)S(1)} fusion(bf16[2,1024,256]{2,1,0:T(8,128)(2,1)} %get-tuple-element.269, f32[2,256,1024]{2,1,0:T(8,128)S(1)} %multiply_reduce_fusion.2, f32[2,256,256]{1,2,0:T(8,128)S(1)} %get-tuple-element.258, pred[]{:T(512)S(6)} %compare.5, bf16[4,256,256]{2,1,0:T(8,128)(2,1)S(1)} %get-tuple-element.270, ...), kind=kOutput, calls=%fused_computation.3.clone.1 | convolution fusion | flops 339083264 | bytes 4325381 | tf_op jit(solution)/shard_map/while/body/eval_jaxpr/while/body/eval_jaxpr/nr,jns->jrs/dot_general | solution.py:56
  129.0 9.3 %fusion.31 = f32[2,256,256]{1,2,0:T(8,128)S(1)} fusion(bf16[2,1024,256]{2,1,0:T(8,128)(2,1)} %get-tuple-element.269, f32[2,256,1024]{2,1,0:T(8,128)S(1)} %multiply_reduce_fusion.2, f32[2,256,256]{1,2,0:T(8,128)S(1)} %get-tuple-element.258, pred[]{:T(512)S(6)} %compare.5, bf16[4,256,256]{2,1,0:T(8,128)(2,1)S(1)} %get-tuple-element.270, ...), kind=kOutput, calls=%fused_computation.3.clone.1 | convolution fusion | flops 339083264 | bytes 4325381 | tf_op jit(solution)/shard_map/while/body/eval_jaxpr/while/body/eval_jaxpr/nr,jns->jrs/dot_general | solution.py:56
  140.5 39.9 %while.24 = (s32[]{:T(128)}, f32[2,256,256]{1,2,0:T(8,128)S(1)}, f32[4,3,256]{2,1,0:T(4,128)S(1)}, f32[2,3,1024]{2,1,0:T(4,128)S(1)}, bf16[2,1024,256]{2,1,0:T(8...) while((s32[]{:T(128)}, f32[2,256,256]{1,2,0:T(8,128)S(1)}, ...), condition=%wide.region_5.5_spmd.clone, body=%wide.region_3.4_spmd.clone.sunk | while | flops 343277568 | bytes 6456423 | solution.py:60
  141.2 9.3 %fusion.31 = f32[2,256,256]{1,2,0:T(8,128)S(1)} fusion(bf16[2,1024,256]{2,1,0:T(8,128)(2,1)} %get-tuple-element.269, f32[2,256,1024]{2,1,0:T(8,128)S(1)} %multiply_reduce_fusion.2, f32[2,256,256]{1,2,0:T(8,128)S(1)} %get-tuple-element.258, pred[]{:T(512)S(6)} %compare.5, bf16[4,256,256]{2,1,0:T(8,128)(2,1)S(1)} %get-tuple-element.270, ...), kind=kOutput, calls=%fused_computation.3.clone.1 | convolution fusion | flops 339083264 | bytes 4325381 | tf_op jit(solution)/shard_map/while/body/eval_jaxpr/while/body/eval_jaxpr/nr,jns->jrs/dot_general | solution.py:56
  151.2 9.3 %fusion.31 = f32[2,256,256]{1,2,0:T(8,128)S(1)} fusion(bf16[2,1024,256]{2,1,0:T(8,128)(2,1)} %get-tuple-element.269, f32[2,256,1024]{2,1,0:T(8,128)S(1)} %multiply_reduce_fusion.2, f32[2,256,256]{1,2,0:T(8,128)S(1)} %get-tuple-element.258, pred[]{:T(512)S(6)} %compare.5, bf16[4,256,256]{2,1,0:T(8,128)(2,1)S(1)} %get-tuple-element.270, ...), kind=kOutput, calls=%fused_computation.3.clone.1 | convolution fusion | flops 339083264 | bytes 4325381 | tf_op jit(solution)/shard_map/while/body/eval_jaxpr/while/body/eval_jaxpr/nr,jns->jrs/dot_general | solution.py:56
  161.1 9.3 %fusion.31 = f32[2,256,256]{1,2,0:T(8,128)S(1)} fusion(bf16[2,1024,256]{2,1,0:T(8,128)(2,1)} %get-tuple-element.269, f32[2,256,1024]{2,1,0:T(8,128)S(1)} %multiply_reduce_fusion.2, f32[2,256,256]{1,2,0:T(8,128)S(1)} %get-tuple-element.258, pred[]{:T(512)S(6)} %compare.5, bf16[4,256,256]{2,1,0:T(8,128)(2,1)S(1)} %get-tuple-element.270, ...), kind=kOutput, calls=%fused_computation.3.clone.1 | convolution fusion | flops 339083264 | bytes 4325381 | tf_op jit(solution)/shard_map/while/body/eval_jaxpr/while/body/eval_jaxpr/nr,jns->jrs/dot_general | solution.py:56
  171.1 9.3 %fusion.31 = f32[2,256,256]{1,2,0:T(8,128)S(1)} fusion(bf16[2,1024,256]{2,1,0:T(8,128)(2,1)} %get-tuple-element.269, f32[2,256,1024]{2,1,0:T(8,128)S(1)} %multiply_reduce_fusion.2, f32[2,256,256]{1,2,0:T(8,128)S(1)} %get-tuple-element.258, pred[]{:T(512)S(6)} %compare.5, bf16[4,256,256]{2,1,0:T(8,128)(2,1)S(1)} %get-tuple-element.270, ...), kind=kOutput, calls=%fused_computation.3.clone.1 | convolution fusion | flops 339083264 | bytes 4325381 | tf_op jit(solution)/shard_map/while/body/eval_jaxpr/while/body/eval_jaxpr/nr,jns->jrs/dot_general | solution.py:56
  182.5 39.9 %while.24 = (s32[]{:T(128)}, f32[2,256,256]{1,2,0:T(8,128)S(1)}, f32[4,3,256]{2,1,0:T(4,128)S(1)}, f32[2,3,1024]{2,1,0:T(4,128)S(1)}, bf16[2,1024,256]{2,1,0:T(8...) while((s32[]{:T(128)}, f32[2,256,256]{1,2,0:T(8,128)S(1)}, ...), condition=%wide.region_5.5_spmd.clone, body=%wide.region_3.4_spmd.clone.sunk | while | flops 343277568 | bytes 6456423 | solution.py:60
  183.2 9.3 %fusion.31 = f32[2,256,256]{1,2,0:T(8,128)S(1)} fusion(bf16[2,1024,256]{2,1,0:T(8,128)(2,1)} %get-tuple-element.269, f32[2,256,1024]{2,1,0:T(8,128)S(1)} %multiply_reduce_fusion.2, f32[2,256,256]{1,2,0:T(8,128)S(1)} %get-tuple-element.258, pred[]{:T(512)S(6)} %compare.5, bf16[4,256,256]{2,1,0:T(8,128)(2,1)S(1)} %get-tuple-element.270, ...), kind=kOutput, calls=%fused_computation.3.clone.1 | convolution fusion | flops 339083264 | bytes 4325381 | tf_op jit(solution)/shard_map/while/body/eval_jaxpr/while/body/eval_jaxpr/nr,jns->jrs/dot_general | solution.py:56
  193.2 9.3 %fusion.31 = f32[2,256,256]{1,2,0:T(8,128)S(1)} fusion(bf16[2,1024,256]{2,1,0:T(8,128)(2,1)} %get-tuple-element.269, f32[2,256,1024]{2,1,0:T(8,128)S(1)} %multiply_reduce_fusion.2, f32[2,256,256]{1,2,0:T(8,128)S(1)} %get-tuple-element.258, pred[]{:T(512)S(6)} %compare.5, bf16[4,256,256]{2,1,0:T(8,128)(2,1)S(1)} %get-tuple-element.270, ...), kind=kOutput, calls=%fused_computation.3.clone.1 | convolution fusion | flops 339083264 | bytes 4325381 | tf_op jit(solution)/shard_map/while/body/eval_jaxpr/while/body/eval_jaxpr/nr,jns->jrs/dot_general | solution.py:56
  203.2 9.3 %fusion.31 = f32[2,256,256]{1,2,0:T(8,128)S(1)} fusion(bf16[2,1024,256]{2,1,0:T(8,128)(2,1)} %get-tuple-element.269, f32[2,256,1024]{2,1,0:T(8,128)S(1)} %multiply_reduce_fusion.2, f32[2,256,256]{1,2,0:T(8,128)S(1)} %get-tuple-element.258, pred[]{:T(512)S(6)} %compare.5, bf16[4,256,256]{2,1,0:T(8,128)(2,1)S(1)} %get-tuple-element.270, ...), kind=kOutput, calls=%fused_computation.3.clone.1 | convolution fusion | flops 339083264 | bytes 4325381 | tf_op jit(solution)/shard_map/while/body/eval_jaxpr/while/body/eval_jaxpr/nr,jns->jrs/dot_general | solution.py:56
  213.2 9.3 %fusion.31 = f32[2,256,256]{1,2,0:T(8,128)S(1)} fusion(bf16[2,1024,256]{2,1,0:T(8,128)(2,1)} %get-tuple-element.269, f32[2,256,1024]{2,1,0:T(8,128)S(1)} %multiply_reduce_fusion.2, f32[2,256,256]{1,2,0:T(8,128)S(1)} %get-tuple-element.258, pred[]{:T(512)S(6)} %compare.5, bf16[4,256,256]{2,1,0:T(8,128)(2,1)S(1)} %get-tuple-element.270, ...), kind=kOutput, calls=%fused_computation.3.clone.1 | convolution fusion | flops 339083264 | bytes 4325381 | tf_op jit(solution)/shard_map/while/body/eval_jaxpr/while/body/eval_jaxpr/nr,jns->jrs/dot_general | solution.py:56
  224.6 39.9 %while.24 = (s32[]{:T(128)}, f32[2,256,256]{1,2,0:T(8,128)S(1)}, f32[4,3,256]{2,1,0:T(4,128)S(1)}, f32[2,3,1024]{2,1,0:T(4,128)S(1)}, bf16[2,1024,256]{2,1,0:T(8...) while((s32[]{:T(128)}, f32[2,256,256]{1,2,0:T(8,128)S(1)}, ...), condition=%wide.region_5.5_spmd.clone, body=%wide.region_3.4_spmd.clone.sunk | while | flops 343277568 | bytes 6456423 | solution.py:60
  225.3 9.3 %fusion.31 = f32[2,256,256]{1,2,0:T(8,128)S(1)} fusion(bf16[2,1024,256]{2,1,0:T(8,128)(2,1)} %get-tuple-element.269, f32[2,256,1024]{2,1,0:T(8,128)S(1)} %multiply_reduce_fusion.2, f32[2,256,256]{1,2,0:T(8,128)S(1)} %get-tuple-element.258, pred[]{:T(512)S(6)} %compare.5, bf16[4,256,256]{2,1,0:T(8,128)(2,1)S(1)} %get-tuple-element.270, ...), kind=kOutput, calls=%fused_computation.3.clone.1 | convolution fusion | flops 339083264 | bytes 4325381 | tf_op jit(solution)/shard_map/while/body/eval_jaxpr/while/body/eval_jaxpr/nr,jns->jrs/dot_general | solution.py:56
  235.3 9.3 %fusion.31 = f32[2,256,256]{1,2,0:T(8,128)S(1)} fusion(bf16[2,1024,256]{2,1,0:T(8,128)(2,1)} %get-tuple-element.269, f32[2,256,1024]{2,1,0:T(8,128)S(1)} %multiply_reduce_fusion.2, f32[2,256,256]{1,2,0:T(8,128)S(1)} %get-tuple-element.258, pred[]{:T(512)S(6)} %compare.5, bf16[4,256,256]{2,1,0:T(8,128)(2,1)S(1)} %get-tuple-element.270, ...), kind=kOutput, calls=%fused_computation.3.clone.1 | convolution fusion | flops 339083264 | bytes 4325381 | tf_op jit(solution)/shard_map/while/body/eval_jaxpr/while/body/eval_jaxpr/nr,jns->jrs/dot_general | solution.py:56
  245.2 9.3 %fusion.31 = f32[2,256,256]{1,2,0:T(8,128)S(1)} fusion(bf16[2,1024,256]{2,1,0:T(8,128)(2,1)} %get-tuple-element.269, f32[2,256,1024]{2,1,0:T(8,128)S(1)} %multiply_reduce_fusion.2, f32[2,256,256]{1,2,0:T(8,128)S(1)} %get-tuple-element.258, pred[]{:T(512)S(6)} %compare.5, bf16[4,256,256]{2,1,0:T(8,128)(2,1)S(1)} %get-tuple-element.270, ...), kind=kOutput, calls=%fused_computation.3.clone.1 | convolution fusion | flops 339083264 | bytes 4325381 | tf_op jit(solution)/shard_map/while/body/eval_jaxpr/while/body/eval_jaxpr/nr,jns->jrs/dot_general | solution.py:56
  255.2 9.3 %fusion.31 = f32[2,256,256]{1,2,0:T(8,128)S(1)} fusion(bf16[2,1024,256]{2,1,0:T(8,128)(2,1)} %get-tuple-element.269, f32[2,256,1024]{2,1,0:T(8,128)S(1)} %multiply_reduce_fusion.2, f32[2,256,256]{1,2,0:T(8,128)S(1)} %get-tuple-element.258, pred[]{:T(512)S(6)} %compare.5, bf16[4,256,256]{2,1,0:T(8,128)(2,1)S(1)} %get-tuple-element.270, ...), kind=kOutput, calls=%fused_computation.3.clone.1 | convolution fusion | flops 339083264 | bytes 4325381 | tf_op jit(solution)/shard_map/while/body/eval_jaxpr/while/body/eval_jaxpr/nr,jns->jrs/dot_general | solution.py:56
  265.5 3.0 broadcast_select_fusion
  270.1 44.8 %all-reduce.7.cloned.1.call-done = bf16[2,2,256,256]{3,2,1,0:T(8,128)(2,1)} async-done(((bf16[2,2,256,256]{3,2,1,0:T(8,128)(2,1)}), bf16[2,2,256,256]{3,2,1,0:T(8,128)(2,1)}) %all-reduce.7.cloned.1.call-update) | async-done | bytes 524304 | tf_op jit(solution)/shard_map/psum | solution.py:16
  314.8 61.6 %all-reduce.9.cloned.1.call-done = bf16[4,2,256,256]{3,2,1,0:T(8,128)(2,1)} async-done(((bf16[4,2,256,256]{3,2,1,0:T(8,128)(2,1)}), bf16[4,2,256,256]{3,2,1,0:T(8,128)(2,1)}) %all-reduce.9.cloned.1.call-update) | async-done | bytes 1048592 | tf_op jit(solution)/shard_map/psum | solution.py:16
  376.5 2.4 fusion.11
  378.9 2.6 convolution_bitcast_fusion.1
  381.5 54.0 %all-reduce.11.cloned.1.call-done = f32[4,64,256]{2,1,0:T(8,128)} async-done(((f32[4,64,256]{2,1,0:T(8,128)}), f32[4,64,256]{2,1,0:T(8,128)}) %all-reduce.11.cloned.1.call-update) | async-done | bytes 262160 | tf_op jit(solution)/shard_map/psum | solution.py:90
  (92 shorter events, 23.9 us)
Async XLA Ops:
  7.2 369.3 %copy-start = (bf16[2,256,256]{2,1,0:T(8,128)(2,1)S(1)}, bf16[2,256,256]{2,1,0:T(8,128)(2,1)}, u32[]{:S(2)}) copy-start(bf16[2,256,256]{2,1,0:T(8,128)(2,1)} %param.12) | copy-start | bytes 786436
  7.2 36.7 %copy-start.4 = (s32[4,3,128]{2,0,1:T(4,128)S(1)}, s32[4,3,128]{2,0,1:T(4,128)}, u32[]{:S(2)}) copy-start(s32[4,3,128]{2,0,1:T(4,128)} %param.9) | copy-start | bytes 18436
  7.2 63.1 %copy-start.5 = (s32[16]{0:T(128)S(1)}, s32[16]{0:T(128)}, u32[]{:S(2)}) copy-start(s32[16]{0:T(128)} %param.10) | copy-start | bytes 196
  7.2 34.3 %all-gather.2.cloned.1.call-start = ((), (), s32[]{:S(2)}) async-start(), calls=%async_computation | async-start | bytes 2359296 | tf_op jit(solution)/shard_map/all_gather | solution.py:31
  7.9 89.4 %all-reduce.5.cloned.1.call-start = ((), (), s32[]{:S(2)}) async-start(), calls=%async_computation.1 | async-start | bytes 2097152 | tf_op jit(solution)/shard_map/psum | solution.py:16
  43.8 271.1 %all-reduce.7.cloned.1.call-start = ((), (), s32[]{:S(2)}) async-start(), calls=%async_computation.2 | async-start | bytes 1048576 | tf_op jit(solution)/shard_map/psum | solution.py:16
  269.3 107.1 %all-reduce.9.cloned.1.call-start = ((), (), s32[]{:S(2)}) async-start(), calls=%async_computation.3 | async-start | bytes 2097152 | tf_op jit(solution)/shard_map/psum | solution.py:16
  269.9 165.6 %all-reduce.11.cloned.1.call-start = ((), (), s32[]{:S(2)}) async-start(), calls=%async_computation.4 | async-start | bytes 524288 | tf_op jit(solution)/shard_map/psum | solution.py:90
  270.1 108.8 %copy-start.1 = (bf16[2,1024,256]{2,1,0:T(8,128)(2,1)S(1)}, bf16[2,1024,256]{2,1,0:T(8,128)(2,1)}, u32[]{:S(2)}) copy-start(bf16[2,1024,256]{2,1,0:T(8,128)(2,1)} %get-tuple-element.313) | copy-start | bytes 3145732
  378.9 58.6 %copy-start.2 = (bf16[4,2,256,256]{3,2,1,0:T(8,128)(2,1)}, bf16[4,2,256,256]{3,2,1,0:T(8,128)(2,1)S(1)}, u32[]{:S(2)}) copy-start(bf16[4,2,256,256]{3,2,1,0:T(8,128)(2,1)S(1)} %fusion.11) | copy-start | bytes 3145732
  378.9 56.6 %copy-start.3 = (bf16[4,128,256]{2,1,0:T(8,128)(2,1)S(1)}, bf16[4,128,256]{2,1,0:T(8,128)(2,1)}, u32[]{:S(2)}) copy-start(bf16[4,128,256]{2,1,0:T(8,128)(2,1)} %param.11) | copy-start | bytes 786436
Sparse Core Ops, SparseCore 0:
  9.6 31.7 all-gather.1
  45.1 52.1 all-reduce.4
  269.5 45.3 all-reduce.6
  317.6 58.8 all-reduce.8
  381.6 53.8 all-reduce.10
where the time goes:
time: 445 us; the launch traced here: 444 us
  waiting for transfers between devices  222 us (50%)
  matrix products  155 us (35%)
  blocking collectives  26.4 us (6%)
  other arithmetic  16.8 us (4%)
  between operations  13.9 us (3%)
  local copies, waits for them, and re-layouts  8.84 us (2%)
    dot_general x16, matrix products, add_block(): jnp.einsum('nr,jns->jrs', block_bases, proj, preferred_element_type=jnp.f...  148 us
    psum x3, waiting for transfers between devices, spread(): return lax.psum(jnp.where(mine, x, jnp.zeros_like(x)), axis)  133 us
    psum x1, waiting for transfers between devices, body(): summed = lax.psum(partial_cores, 'col')  54 us
    all_gather x1, waiting for transfers between devices, body(): lax.all_gather(bases, 'col', axis=1, tiled=True)  33.5 us
    psum x1, blocking collectives, spread(): return lax.psum(jnp.where(mine, x, jnp.zeros_like(x)), axis)  16 us
    reduce_sum x16, other arithmetic, kernel_block(): dist = jnp.sqrt(jnp.sum(diff * diff, axis=0) + nugget)  10.5 us
    all_gather x1, blocking collectives, body(): lax.all_gather(points.astype(jnp.bfloat16), 'col', axis=2, tiled=True)  10.4 us
  transfers between devices with their start and end apart: 5, of which 5 were waited for; matrix products, arithmetic and copies ran while one was open for 0% of the time, Pallas kernels for 0%

commit v1 on v0

--- a/solution.py
+++ b/solution.py
@@ -87,7 +87,8 @@
     partial_cores = jnp.einsum(
         "ijab,jpb->ipa", updated, probe_cores, preferred_element_type=jnp.float32
     )
-    summed = lax.psum(partial_cores, "col")
+    pieces = lax.all_gather(partial_cores, "col")
+    summed = jnp.sum(pieces, axis=0)
     images = jnp.einsum(
         "ipa,ina->ipn", summed, bases.astype(jnp.float32), precision=lax.Precision.HIGHEST
     )

time: 445 us -> 420 us (0.944)
  waiting for transfers between devices: 222 us -> 196 us
    psum x1 -> x0, waiting for transfers between devices: 54 us -> none  [body(): summed = lax.psum(partial_cores, 'col')]
    all_gather x0 -> x1, waiting for transfers between devices: none -> 28.2 us  [body(): pieces = lax.all_gather(partial_cores, 'col')]
where the time goes in v1:
time: 420 us; the launch traced here: 419 us
  waiting for transfers between devices  196 us (47%)
  matrix products  154 us (37%)
  blocking collectives  26.4 us (6%)
  other arithmetic  18.6 us (4%)
  between operations  13.9 us (3%)
  local copies, waits for them, and re-layouts  8.84 us (2%)
    dot_general x16, matrix products, add_block(): jnp.einsum('nr,jns->jrs', block_bases, proj, preferred_element_type=jnp.f...  148 us
    psum x3, waiting for transfers between devices, spread(): return lax.psum(jnp.where(mine, x, jnp.zeros_like(x)), axis)  133 us
    all_gather x1, waiting for transfers between devices, body(): lax.all_gather(bases, 'col', axis=1, tiled=True)  33.5 us
    all_gather x1, waiting for transfers between devices, body(): pieces = lax.all_gather(partial_cores, 'col')  28.2 us
    psum x1, blocking collectives, spread(): return lax.psum(jnp.where(mine, x, jnp.zeros_like(x)), axis)  16 us
    reduce_sum x16, other arithmetic, kernel_block(): dist = jnp.sqrt(jnp.sum(diff * diff, axis=0) + nugget)  10.5 us
    all_gather x1, blocking collectives, body(): lax.all_gather(points.astype(jnp.bfloat16), 'col', axis=2, tiled=True)  10.4 us
  transfers between devices with their start and end apart: 5, of which 5 were waited for; matrix products, arithmetic and copies ran while one was open for 0% of the time, Pallas kernels for 0%

profile of v1, /device:TPU:0, one launch (start us, length us, event | category | flops | bytes accessed | tf_op | source)
XLA Modules:
  0.0 419.0 jit_solution(7669399850159658707)
XLA Ops:
  8.0 33.5 %all-gather.4.cloned.1.call-done = bf16[4,1024,256]{2,1,0:T(8,128)(2,1)} async-done(((bf16[4,128,256]{2,1,0:T(8,128)(2,1)}), bf16[4,1024,256]{2,1,0:T(8,128)(2,1)}) %all-gather.4.cloned.1.call-update) | async-done | bytes 2097168 | tf_op jit(solution)/shard_map/all_gather | solution.py:31
  41.5 2.3 dynamic-slice_select_fusion
  43.9 10.4 %all_gather.12 = bf16[4,3,1024]{2,0,1:T(4,128)(2,1)S(1)} all-gather(bf16[4,3,128]{2,0,1:T(4,128)(2,1)S(1)} %convert_element_type.53), channel_id=1, replica_groups=mesh['row'=4,'col'=8] {'col'}, dimensions={2}, use_global_device_ids=true | all-gather | bytes 27648 | tf_op jit(solution)/shard_map/all_gather | solution.py:32
  54.3 16.0 %psum.28 = bf16[2,3,1024]{2,0,1:T(2,128)(2,1)S(1)} all-reduce(bf16[2,3,1024]{2,0,1:T(2,128)(2,1)S(1)} %broadcast_select_fusion.1), channel_id=1, replica_groups=mesh['row'=4,'col'=8] {'row'}, use_global_device_ids=true, to_apply=%region_0.1 | all-reduce | flops 6144 | bytes 24576 | tf_op jit(solution)/shard_map/psum | solution.py:16
  70.6 26.7 %all-reduce.4.cloned.1.call-done = bf16[2,1024,256]{2,1,0:T(8,128)(2,1)} async-done(((bf16[2,1024,256]{2,1,0:T(8,128)(2,1)}), bf16[2,1024,256]{2,1,0:T(8,128)(2,1)}) %all-reduce.4.cloned.1.call-update) | async-done | bytes 1048592 | tf_op jit(solution)/shard_map/psum | solution.py:16
  97.3 168.2 %while.25 = (s32[]{:T(128)}, f32[4,2,256,256]{3,2,1,0:T(8,128)}, bf16[4,3,1024]{2,1,0:T(4,128)(2,1)S(1)}, bf16[4,1024,256]{2,1,0:T(8,128)(2,1)}, f32[2,3,1024]{2...) while((s32[]{:T(128)}, f32[4,2,256,256]{3,2,1,0:T(8,128)}, ...), condition=%wide.region_6.7_spmd.clone, body=%wide.region_2.6_spmd.sunk.clone | while | flops 343280640 | bytes 9633548 | solution.py:65
  98.4 39.9 %while.24 = (s32[]{:T(128)}, f32[2,256,256]{1,2,0:T(8,128)S(1)}, f32[4,3,256]{2,1,0:T(4,128)S(1)}, f32[2,3,1024]{2,1,0:T(4,128)S(1)}, bf16[2,1024,256]{2,1,0:T(8...) while((s32[]{:T(128)}, f32[2,256,256]{1,2,0:T(8,128)S(1)}, ...), condition=%wide.region_5.5_spmd.clone, body=%wide.region_3.4_spmd.clone.sunk | while | flops 343277568 | bytes 6456423 | solution.py:60
  99.1 9.3 %fusion.31 = f32[2,256,256]{1,2,0:T(8,128)S(1)} fusion(bf16[2,1024,256]{2,1,0:T(8,128)(2,1)} %get-tuple-element.275, f32[2,256,1024]{2,1,0:T(8,128)S(1)} %multiply_reduce_fusion.2, f32[2,256,256]{1,2,0:T(8,128)S(1)} %get-tuple-element.264, pred[]{:T(512)S(6)} %compare.5, bf16[4,256,256]{2,1,0:T(8,128)(2,1)S(1)} %get-tuple-element.276, ...), kind=kOutput, calls=%fused_computation.3.clone.1 | convolution fusion | flops 339083264 | bytes 4325381 | tf_op jit(solution)/shard_map/while/body/eval_jaxpr/while/body/eval_jaxpr/nr,jns->jrs/dot_general | solution.py:56
  109.1 9.3 %fusion.31 = f32[2,256,256]{1,2,0:T(8,128)S(1)} fusion(bf16[2,1024,256]{2,1,0:T(8,128)(2,1)} %get-tuple-element.275, f32[2,256,1024]{2,1,0:T(8,128)S(1)} %multiply_reduce_fusion.2, f32[2,256,256]{1,2,0:T(8,128)S(1)} %get-tuple-element.264, pred[]{:T(512)S(6)} %compare.5, bf16[4,256,256]{2,1,0:T(8,128)(2,1)S(1)} %get-tuple-element.276, ...), kind=kOutput, calls=%fused_computation.3.clone.1 | convolution fusion | flops 339083264 | bytes 4325381 | tf_op jit(solution)/shard_map/while/body/eval_jaxpr/while/body/eval_jaxpr/nr,jns->jrs/dot_general | solution.py:56
  119.1 9.3 %fusion.31 = f32[2,256,256]{1,2,0:T(8,128)S(1)} fusion(bf16[2,1024,256]{2,1,0:T(8,128)(2,1)} %get-tuple-element.275, f32[2,256,1024]{2,1,0:T(8,128)S(1)} %multiply_reduce_fusion.2, f32[2,256,256]{1,2,0:T(8,128)S(1)} %get-tuple-element.264, pred[]{:T(512)S(6)} %compare.5, bf16[4,256,256]{2,1,0:T(8,128)(2,1)S(1)} %get-tuple-element.276, ...), kind=kOutput, calls=%fused_computation.3.clone.1 | convolution fusion | flops 339083264 | bytes 4325381 | tf_op jit(solution)/shard_map/while/body/eval_jaxpr/while/body/eval_jaxpr/nr,jns->jrs/dot_general | solution.py:56
  129.1 9.3 %fusion.31 = f32[2,256,256]{1,2,0:T(8,128)S(1)} fusion(bf16[2,1024,256]{2,1,0:T(8,128)(2,1)} %get-tuple-element.275, f32[2,256,1024]{2,1,0:T(8,128)S(1)} %multiply_reduce_fusion.2, f32[2,256,256]{1,2,0:T(8,128)S(1)} %get-tuple-element.264, pred[]{:T(512)S(6)} %compare.5, bf16[4,256,256]{2,1,0:T(8,128)(2,1)S(1)} %get-tuple-element.276, ...), kind=kOutput, calls=%fused_computation.3.clone.1 | convolution fusion | flops 339083264 | bytes 4325381 | tf_op jit(solution)/shard_map/while/body/eval_jaxpr/while/body/eval_jaxpr/nr,jns->jrs/dot_general | solution.py:56
  140.5 39.9 %while.24 = (s32[]{:T(128)}, f32[2,256,256]{1,2,0:T(8,128)S(1)}, f32[4,3,256]{2,1,0:T(4,128)S(1)}, f32[2,3,1024]{2,1,0:T(4,128)S(1)}, bf16[2,1024,256]{2,1,0:T(8...) while((s32[]{:T(128)}, f32[2,256,256]{1,2,0:T(8,128)S(1)}, ...), condition=%wide.region_5.5_spmd.clone, body=%wide.region_3.4_spmd.clone.sunk | while | flops 343277568 | bytes 6456423 | solution.py:60
  141.2 9.3 %fusion.31 = f32[2,256,256]{1,2,0:T(8,128)S(1)} fusion(bf16[2,1024,256]{2,1,0:T(8,128)(2,1)} %get-tuple-element.275, f32[2,256,1024]{2,1,0:T(8,128)S(1)} %multiply_reduce_fusion.2, f32[2,256,256]{1,2,0:T(8,128)S(1)} %get-tuple-element.264, pred[]{:T(512)S(6)} %compare.5, bf16[4,256,256]{2,1,0:T(8,128)(2,1)S(1)} %get-tuple-element.276, ...), kind=kOutput, calls=%fused_computation.3.clone.1 | convolution fusion | flops 339083264 | bytes 4325381 | tf_op jit(solution)/shard_map/while/body/eval_jaxpr/while/body/eval_jaxpr/nr,jns->jrs/dot_general | solution.py:56
  151.2 9.3 %fusion.31 = f32[2,256,256]{1,2,0:T(8,128)S(1)} fusion(bf16[2,1024,256]{2,1,0:T(8,128)(2,1)} %get-tuple-element.275, f32[2,256,1024]{2,1,0:T(8,128)S(1)} %multiply_reduce_fusion.2, f32[2,256,256]{1,2,0:T(8,128)S(1)} %get-tuple-element.264, pred[]{:T(512)S(6)} %compare.5, bf16[4,256,256]{2,1,0:T(8,128)(2,1)S(1)} %get-tuple-element.276, ...), kind=kOutput, calls=%fused_computation.3.clone.1 | convolution fusion | flops 339083264 | bytes 4325381 | tf_op jit(solution)/shard_map/while/body/eval_jaxpr/while/body/eval_jaxpr/nr,jns->jrs/dot_general | solution.py:56
  161.1 9.3 %fusion.31 = f32[2,256,256]{1,2,0:T(8,128)S(1)} fusion(bf16[2,1024,256]{2,1,0:T(8,128)(2,1)} %get-tuple-element.275, f32[2,256,1024]{2,1,0:T(8,128)S(1)} %multiply_reduce_fusion.2, f32[2,256,256]{1,2,0:T(8,128)S(1)} %get-tuple-element.264, pred[]{:T(512)S(6)} %compare.5, bf16[4,256,256]{2,1,0:T(8,128)(2,1)S(1)} %get-tuple-element.276, ...), kind=kOutput, calls=%fused_computation.3.clone.1 | convolution fusion | flops 339083264 | bytes 4325381 | tf_op jit(solution)/shard_map/while/body/eval_jaxpr/while/body/eval_jaxpr/nr,jns->jrs/dot_general | solution.py:56
  171.1 9.3 %fusion.31 = f32[2,256,256]{1,2,0:T(8,128)S(1)} fusion(bf16[2,1024,256]{2,1,0:T(8,128)(2,1)} %get-tuple-element.275, f32[2,256,1024]{2,1,0:T(8,128)S(1)} %multiply_reduce_fusion.2, f32[2,256,256]{1,2,0:T(8,128)S(1)} %get-tuple-element.264, pred[]{:T(512)S(6)} %compare.5, bf16[4,256,256]{2,1,0:T(8,128)(2,1)S(1)} %get-tuple-element.276, ...), kind=kOutput, calls=%fused_computation.3.clone.1 | convolution fusion | flops 339083264 | bytes 4325381 | tf_op jit(solution)/shard_map/while/body/eval_jaxpr/while/body/eval_jaxpr/nr,jns->jrs/dot_general | solution.py:56
  182.6 39.9 %while.24 = (s32[]{:T(128)}, f32[2,256,256]{1,2,0:T(8,128)S(1)}, f32[4,3,256]{2,1,0:T(4,128)S(1)}, f32[2,3,1024]{2,1,0:T(4,128)S(1)}, bf16[2,1024,256]{2,1,0:T(8...) while((s32[]{:T(128)}, f32[2,256,256]{1,2,0:T(8,128)S(1)}, ...), condition=%wide.region_5.5_spmd.clone, body=%wide.region_3.4_spmd.clone.sunk | while | flops 343277568 | bytes 6456423 | solution.py:60
  183.3 9.3 %fusion.31 = f32[2,256,256]{1,2,0:T(8,128)S(1)} fusion(bf16[2,1024,256]{2,1,0:T(8,128)(2,1)} %get-tuple-element.275, f32[2,256,1024]{2,1,0:T(8,128)S(1)} %multiply_reduce_fusion.2, f32[2,256,256]{1,2,0:T(8,128)S(1)} %get-tuple-element.264, pred[]{:T(512)S(6)} %compare.5, bf16[4,256,256]{2,1,0:T(8,128)(2,1)S(1)} %get-tuple-element.276, ...), kind=kOutput, calls=%fused_computation.3.clone.1 | convolution fusion | flops 339083264 | bytes 4325381 | tf_op jit(solution)/shard_map/while/body/eval_jaxpr/while/body/eval_jaxpr/nr,jns->jrs/dot_general | solution.py:56
  193.2 9.3 %fusion.31 = f32[2,256,256]{1,2,0:T(8,128)S(1)} fusion(bf16[2,1024,256]{2,1,0:T(8,128)(2,1)} %get-tuple-element.275, f32[2,256,1024]{2,1,0:T(8,128)S(1)} %multiply_reduce_fusion.2, f32[2,256,256]{1,2,0:T(8,128)S(1)} %get-tuple-element.264, pred[]{:T(512)S(6)} %compare.5, bf16[4,256,256]{2,1,0:T(8,128)(2,1)S(1)} %get-tuple-element.276, ...), kind=kOutput, calls=%fused_computation.3.clone.1 | convolution fusion | flops 339083264 | bytes 4325381 | tf_op jit(solution)/shard_map/while/body/eval_jaxpr/while/body/eval_jaxpr/nr,jns->jrs/dot_general | solution.py:56
  203.2 9.3 %fusion.31 = f32[2,256,256]{1,2,0:T(8,128)S(1)} fusion(bf16[2,1024,256]{2,1,0:T(8,128)(2,1)} %get-tuple-element.275, f32[2,256,1024]{2,1,0:T(8,128)S(1)} %multiply_reduce_fusion.2, f32[2,256,256]{1,2,0:T(8,128)S(1)} %get-tuple-element.264, pred[]{:T(512)S(6)} %compare.5, bf16[4,256,256]{2,1,0:T(8,128)(2,1)S(1)} %get-tuple-element.276, ...), kind=kOutput, calls=%fused_computation.3.clone.1 | convolution fusion | flops 339083264 | bytes 4325381 | tf_op jit(solution)/shard_map/while/body/eval_jaxpr/while/body/eval_jaxpr/nr,jns->jrs/dot_general | solution.py:56
  213.2 9.3 %fusion.31 = f32[2,256,256]{1,2,0:T(8,128)S(1)} fusion(bf16[2,1024,256]{2,1,0:T(8,128)(2,1)} %get-tuple-element.275, f32[2,256,1024]{2,1,0:T(8,128)S(1)} %multiply_reduce_fusion.2, f32[2,256,256]{1,2,0:T(8,128)S(1)} %get-tuple-element.264, pred[]{:T(512)S(6)} %compare.5, bf16[4,256,256]{2,1,0:T(8,128)(2,1)S(1)} %get-tuple-element.276, ...), kind=kOutput, calls=%fused_computation.3.clone.1 | convolution fusion | flops 339083264 | bytes 4325381 | tf_op jit(solution)/shard_map/while/body/eval_jaxpr/while/body/eval_jaxpr/nr,jns->jrs/dot_general | solution.py:56
  224.6 39.9 %while.24 = (s32[]{:T(128)}, f32[2,256,256]{1,2,0:T(8,128)S(1)}, f32[4,3,256]{2,1,0:T(4,128)S(1)}, f32[2,3,1024]{2,1,0:T(4,128)S(1)}, bf16[2,1024,256]{2,1,0:T(8...) while((s32[]{:T(128)}, f32[2,256,256]{1,2,0:T(8,128)S(1)}, ...), condition=%wide.region_5.5_spmd.clone, body=%wide.region_3.4_spmd.clone.sunk | while | flops 343277568 | bytes 6456423 | solution.py:60
  225.3 9.3 %fusion.31 = f32[2,256,256]{1,2,0:T(8,128)S(1)} fusion(bf16[2,1024,256]{2,1,0:T(8,128)(2,1)} %get-tuple-element.275, f32[2,256,1024]{2,1,0:T(8,128)S(1)} %multiply_reduce_fusion.2, f32[2,256,256]{1,2,0:T(8,128)S(1)} %get-tuple-element.264, pred[]{:T(512)S(6)} %compare.5, bf16[4,256,256]{2,1,0:T(8,128)(2,1)S(1)} %get-tuple-element.276, ...), kind=kOutput, calls=%fused_computation.3.clone.1 | convolution fusion | flops 339083264 | bytes 4325381 | tf_op jit(solution)/shard_map/while/body/eval_jaxpr/while/body/eval_jaxpr/nr,jns->jrs/dot_general | solution.py:56
  235.3 9.3 %fusion.31 = f32[2,256,256]{1,2,0:T(8,128)S(1)} fusion(bf16[2,1024,256]{2,1,0:T(8,128)(2,1)} %get-tuple-element.275, f32[2,256,1024]{2,1,0:T(8,128)S(1)} %multiply_reduce_fusion.2, f32[2,256,256]{1,2,0:T(8,128)S(1)} %get-tuple-element.264, pred[]{:T(512)S(6)} %compare.5, bf16[4,256,256]{2,1,0:T(8,128)(2,1)S(1)} %get-tuple-element.276, ...), kind=kOutput, calls=%fused_computation.3.clone.1 | convolution fusion | flops 339083264 | bytes 4325381 | tf_op jit(solution)/shard_map/while/body/eval_jaxpr/while/body/eval_jaxpr/nr,jns->jrs/dot_general | solution.py:56
  245.3 9.3 %fusion.31 = f32[2,256,256]{1,2,0:T(8,128)S(1)} fusion(bf16[2,1024,256]{2,1,0:T(8,128)(2,1)} %get-tuple-element.275, f32[2,256,1024]{2,1,0:T(8,128)S(1)} %multiply_reduce_fusion.2, f32[2,256,256]{1,2,0:T(8,128)S(1)} %get-tuple-element.264, pred[]{:T(512)S(6)} %compare.5, bf16[4,256,256]{2,1,0:T(8,128)(2,1)S(1)} %get-tuple-element.276, ...), kind=kOutput, calls=%fused_computation.3.clone.1 | convolution fusion | flops 339083264 | bytes 4325381 | tf_op jit(solution)/shard_map/while/body/eval_jaxpr/while/body/eval_jaxpr/nr,jns->jrs/dot_general | solution.py:56
  255.2 9.3 %fusion.31 = f32[2,256,256]{1,2,0:T(8,128)S(1)} fusion(bf16[2,1024,256]{2,1,0:T(8,128)(2,1)} %get-tuple-element.275, f32[2,256,1024]{2,1,0:T(8,128)S(1)} %multiply_reduce_fusion.2, f32[2,256,256]{1,2,0:T(8,128)S(1)} %get-tuple-element.264, pred[]{:T(512)S(6)} %compare.5, bf16[4,256,256]{2,1,0:T(8,128)(2,1)S(1)} %get-tuple-element.276, ...), kind=kOutput, calls=%fused_computation.3.clone.1 | convolution fusion | flops 339083264 | bytes 4325381 | tf_op jit(solution)/shard_map/while/body/eval_jaxpr/while/body/eval_jaxpr/nr,jns->jrs/dot_general | solution.py:56
  265.6 2.9 broadcast_select_fusion
  270.1 44.8 %all-reduce.6.cloned.1.call-done = bf16[2,2,256,256]{3,2,1,0:T(8,128)(2,1)} async-done(((bf16[2,2,256,256]{3,2,1,0:T(8,128)(2,1)}), bf16[2,2,256,256]{3,2,1,0:T(8,128)(2,1)}) %all-reduce.6.cloned.1.call-update) | async-done | bytes 524304 | tf_op jit(solution)/shard_map/psum | solution.py:16
  314.8 61.6 %all-reduce.8.cloned.1.call-done = bf16[4,2,256,256]{3,2,1,0:T(8,128)(2,1)} async-done(((bf16[4,2,256,256]{3,2,1,0:T(8,128)(2,1)}), bf16[4,2,256,256]{3,2,1,0:T(8,128)(2,1)}) %all-reduce.8.cloned.1.call-update) | async-done | bytes 1048592 | tf_op jit(solution)/shard_map/psum | solution.py:16
  376.5 2.4 fusion.11
  378.9 2.6 convolution_bitcast_fusion.1
  381.5 28.2 %all-gather.6.cloned.1.call-done = f32[32,64,256]{2,1,0:T(8,128)} async-done(((f32[4,64,256]{2,1,0:T(8,128)}), f32[32,64,256]{2,1,0:T(8,128)}) %all-gather.6.cloned.1.call-update) | async-done | bytes 2097168 | tf_op jit(solution)/shard_map/all_gather | solution.py:90
  (93 shorter events, 24.7 us)
Async XLA Ops:
  7.2 369.3 %copy-start = (bf16[2,256,256]{2,1,0:T(8,128)(2,1)S(1)}, bf16[2,256,256]{2,1,0:T(8,128)(2,1)}, u32[]{:S(2)}) copy-start(bf16[2,256,256]{2,1,0:T(8,128)(2,1)} %param.12) | copy-start | bytes 786436
  7.2 36.7 %copy-start.4 = (s32[4,3,128]{2,0,1:T(4,128)S(1)}, s32[4,3,128]{2,0,1:T(4,128)}, u32[]{:S(2)}) copy-start(s32[4,3,128]{2,0,1:T(4,128)} %param.9) | copy-start | bytes 18436
  7.2 63.1 %copy-start.5 = (s32[16]{0:T(128)S(1)}, s32[16]{0:T(128)}, u32[]{:S(2)}) copy-start(s32[16]{0:T(128)} %param.10) | copy-start | bytes 196
  7.2 34.3 %all-gather.4.cloned.1.call-start = ((), (), s32[]{:S(2)}) async-start(), calls=%async_computation | async-start | bytes 2359296 | tf_op jit(solution)/shard_map/all_gather | solution.py:31
  7.9 89.4 %all-reduce.4.cloned.1.call-start = ((), (), s32[]{:S(2)}) async-start(), calls=%async_computation.1 | async-start | bytes 2097152 | tf_op jit(solution)/shard_map/psum | solution.py:16
  43.8 271.1 %all-reduce.6.cloned.1.call-start = ((), (), s32[]{:S(2)}) async-start(), calls=%async_computation.2 | async-start | bytes 1048576 | tf_op jit(solution)/shard_map/psum | solution.py:16
  269.4 107.1 %all-reduce.8.cloned.1.call-start = ((), (), s32[]{:S(2)}) async-start(), calls=%async_computation.3 | async-start | bytes 2097152 | tf_op jit(solution)/shard_map/psum | solution.py:16
  269.9 139.8 %all-gather.6.cloned.1.call-start = ((), (), s32[]{:S(2)}) async-start(), calls=%async_computation.4 | async-start | bytes 2359296 | tf_op jit(solution)/shard_map/all_gather | solution.py:90
  270.1 108.8 %copy-start.1 = (bf16[2,1024,256]{2,1,0:T(8,128)(2,1)S(1)}, bf16[2,1024,256]{2,1,0:T(8,128)(2,1)}, u32[]{:S(2)}) copy-start(bf16[2,1024,256]{2,1,0:T(8,128)(2,1)} %get-tuple-element.320) | copy-start | bytes 3145732
  378.9 32.6 %copy-start.2 = (bf16[4,2,256,256]{3,2,1,0:T(8,128)(2,1)}, bf16[4,2,256,256]{3,2,1,0:T(8,128)(2,1)S(1)}, u32[]{:S(2)}) copy-start(bf16[4,2,256,256]{3,2,1,0:T(8,128)(2,1)S(1)} %fusion.11) | copy-start | bytes 3145732
  378.9 32.6 %copy-start.3 = (bf16[4,128,256]{2,1,0:T(8,128)(2,1)S(1)}, bf16[4,128,256]{2,1,0:T(8,128)(2,1)}, u32[]{:S(2)}) copy-start(bf16[4,128,256]{2,1,0:T(8,128)(2,1)} %param.11) | copy-start | bytes 786436
Sparse Core Ops, SparseCore 0:
  9.6 31.7 all-gather.3
  45.1 52.1 all-reduce.3
  269.5 45.3 all-reduce.5
  317.6 58.8 all-reduce.7
  381.6 28.0 all-gather.5
